TPU v7x, 32 devices: a whole 2x2x4 slice. The times are simulated.
32 devices in a mesh: row: 4 (over y, x), col: 8 (over z, core).
Axes of the slice: x: 2, y: 2, z: 4, core: 2. Of those that a mesh axis runs over, the one named last changes fastest.
Arguments:
- queries: bfloat16 [2, 64, 128, 2240], P(None, 'row', 'col'), may hold values from -6 to 6
- key_rows_per_head: bfloat16 [2, 64, 128, 2240], P(None, 'row', 'col'), may hold values from -1000 to 1000
- value_rows_per_head: bfloat16 [2, 64, 128, 2240], P(None, 'row', 'col'), may hold values from -13 to 13
- latent_projection_weight: bfloat16 [2240, 32], replicated, may hold values from -0.125 to 0.125
- entry_conv_weight: bfloat16 [3, 3, 32, 512], replicated, may hold values from -0.375 to 0.375
- residual_norm_gain: float32 [512], replicated, may hold values from 0.1 to 1.9
- residual_conv_weight: bfloat16 [3, 3, 512, 512], replicated, may hold values from -0.09375 to 0.09375
- upscale_conv_weight: bfloat16 [3, 3, 512, 512], replicated, may hold values from -0.09375 to 0.09375
Outputs:
- decoded_image: bfloat16 [2, 128, 256, 512], P(None, 'row', 'col')
All inputs are finite; a program needn't handle non-finite values.
Results may differ from a plain program's by a relative error of at most 0.017.
Values may be sent and summed in bfloat16 or wider, within the bound.
A program may use at most 128 MiB of HBM per device.

v0:
```python
import functools

import jax
import jax.numpy as jnp
from jax import lax
from jax.experimental import pallas as pl
from jax.experimental.pallas import tpu as pltpu
from jax.sharding import PartitionSpec as P

HEAD = 32
NORM_EPS = 1e-06
LANES = 128
HALO = 3
SLOT = 24
MESH = pl.DeviceIdType.MESH
F32 = jnp.float32
BF16 = jnp.bfloat16
AROUND = ((-1, -1), (-1, 0), (-1, 1), (0, -1), (0, 1), (1, -1), (1, 0), (1, 1))


def contract(a, b, dim_a, dim_b):
    return lax.dot_general(a, b, (((dim_a,), (dim_b,)), ((), ())), preferred_element_type=F32)


def same_head(shape):
    return lax.broadcasted_iota(jnp.int32, shape, 0) // HEAD == lax.broadcasted_iota(
        jnp.int32, shape, 1
    ) // HEAD


def attention_kernel(
    rows, cols, tile, width, per_chip,
    k_hbm, v_hbm, q_hbm, proj_hbm, ext_ref,
    k_buf, v_buf, q_buf, proj, part, other, chip_sum, arrived, total, lat, strips, halo,
    in_sem, swap_sem, rs_send, rs_recv, ag_send, ag_recv, halo_send, halo_recv,
):
    row, col = lax.axis_index("row"), lax.axis_index("col")
    core = lax.rem(col, 2)
    zs = cols // 2
    chips = rows * zs
    chip = row * zs + col // 2
    me = row * cols + col
    tokens = tile * tile
    blocks = -(-width // LANES)
    token_count = float(tokens * rows * cols)

    def place(c):
        return (c // zs, lax.rem(c, zs) * 2 + core)

    partner = (row, col + 1 - 2 * core)

    loads = {}
    for step in range(2):
        image = (1 - core) if step == 0 else core
        loads["k", step] = pltpu.make_async_copy(k_hbm.at[image], k_buf.at[image], in_sem.at[step])
        loads["v", step] = pltpu.make_async_copy(v_hbm.at[image], v_buf.at[image], in_sem.at[2 + step])
    load_proj = pltpu.make_async_copy(proj_hbm, proj, in_sem.at[4])
    load_q = pltpu.make_async_copy(q_hbm, q_buf, in_sem.at[5])
    for copy in loads.values():
        copy.start()
    load_proj.start()
    load_q.start()

    barrier = pltpu.get_barrier_semaphore()

    def greet(d, carry):
        t = lax.rem(me + d, rows * cols)
        pl.semaphore_signal(
            barrier, inc=1, device_id=(t // cols, lax.rem(t, cols)), device_id_type=MESH
        )
        return carry

    lax.fori_loop(1, rows * cols, greet, 0)

    units = chips * per_chip
    part[:, 2 * blocks :] = jnp.zeros((2, units - 2 * blocks, 16, LANES), F32)
    mask = same_head((LANES, LANES))

    def sums(image):
        for b in range(blocks):
            lo = b * LANES
            w = min(LANES, width - lo)
            keys = jnp.maximum(k_buf[image, :, lo : lo + w], 0)
            values = v_buf[image, :, lo : lo + w]
            full = jnp.where(mask[:w, :w], contract(values, keys, 0, 0), 0.0)
            packed = full[0:HEAD]
            for h in range(1, w // HEAD):
                packed = packed + full[h * HEAD : (h + 1) * HEAD]
            mean = jnp.sum(keys.astype(F32), axis=0, keepdims=True)
            part[image, 2 * b, :, 0:w] = packed[0:16]
            part[image, 2 * b + 1, :, 0:w] = packed[16:32]
            part[image, 2 * blocks + b // 16, b % 16 : b % 16 + 1, 0:w] = mean

    loads["k", 0].wait()
    loads["v", 0].wait()
    sums(1 - core)
    pl.semaphore_wait(barrier, rows * cols - 1)
    swap = pltpu.make_async_remote_copy(
        src_ref=part.at[1 - core], dst_ref=other, send_sem=swap_sem.at[0],
        recv_sem=swap_sem.at[1], device_id=partner, device_id_type=MESH,
    )
    swap.start()
    loads["k", 1].wait()
    loads["v", 1].wait()
    sums(core)
    swap.wait()
    chip_sum[...] = (part[core] + other[...]).reshape(chips, per_chip, 16, LANES).astype(BF16)

    def scatter(k):
        t = lax.rem(chip + k, chips)
        return pltpu.make_async_remote_copy(
            src_ref=chip_sum.at[t], dst_ref=arrived.at[chip], send_sem=rs_send.at[k],
            recv_sem=rs_recv.at[chip], device_id=place(t), device_id_type=MESH,
        )

    def scatter_from(k):
        t = lax.rem(chip + k, chips)
        return t, pltpu.make_async_remote_copy(
            src_ref=chip_sum.at[t], dst_ref=arrived.at[t], send_sem=rs_send.at[k],
            recv_sem=rs_recv.at[t], device_id=place(t), device_id_type=MESH,
        )

    def gather(k):
        t = lax.rem(chip + k, chips)
        return pltpu.make_async_remote_copy(
            src_ref=total.at[core, chip], dst_ref=total.at[core, chip], send_sem=ag_send.at[k],
            recv_sem=ag_recv.at[chip], device_id=place(t), device_id_type=MESH,
        )

    def gather_from(k):
        t = lax.rem(chip + k, chips)
        return pltpu.make_async_remote_copy(
            src_ref=total.at[core, t], dst_ref=total.at[core, t], send_sem=ag_send.at[k],
            recv_sem=ag_recv.at[t], device_id=place(t), device_id_type=MESH,
        )

    def each(body):
        def step(k, carry):
            body(k)
            return carry

        lax.fori_loop(1, chips, step, 0)

    each(lambda k: scatter(k).start())

    def add(k, acc):
        t, copy = scatter_from(k)
        copy.wait_recv()
        return acc + arrived[t].astype(F32)

    acc = lax.fori_loop(1, chips, add, chip_sum[chip].astype(F32))
    total[core, chip] = (acc / token_count).astype(BF16)
    each(lambda k: gather(k).start())
    each(lambda k: gather_from(k).wait_recv())
    swap_back = pltpu.make_async_remote_copy(
        src_ref=total.at[core], dst_ref=total.at[core], send_sem=swap_sem.at[2],
        recv_sem=swap_sem.at[3], device_id=partner, device_id_type=MESH,
    )
    swap_back.start()
    load_q.wait()
    load_proj.wait()

    def unit(image, u, lo=0, hi=16):
        return total[image, u // per_chip, u % per_chip]

    def attend(image):
        squares = jnp.zeros((tokens, 1), F32)
        out = jnp.zeros((tokens, HEAD), F32)
        means = [
            unit(image, 2 * blocks + i).astype(F32) for i in range(-(-blocks // 16))
        ]
        for b in range(blocks):
            lo = b * LANES
            w = min(LANES, width - lo)
            packed = jnp.concatenate(
                [unit(image, 2 * b).astype(F32), unit(image, 2 * b + 1).astype(F32)], axis=0
            )
            spread = jnp.where(mask, jnp.concatenate([packed] * (LANES // HEAD), axis=0), 0.0)
            mean = means[b // 16][b % 16 : b % 16 + 1]
            spread_mean = jnp.where(mask, jnp.broadcast_to(mean, (LANES, LANES)), 0.0)
            both = jnp.concatenate([spread, spread_mean], axis=0).astype(BF16)
            query = jnp.maximum(q_buf[image, :, lo : lo + w], 0)
            result = contract(query, both[:, :w], 1, 1)
            attended = result[:, :w] / jnp.maximum(result[:, LANES : LANES + w], 1.0)
            squares = squares + jnp.sum(attended * attended, axis=1, keepdims=True)
            out = out + contract(attended.astype(BF16), proj[:, lo : lo + w], 1, 1)
        out = out * lax.rsqrt(squares / width + NORM_EPS)
        out = out.astype(BF16).astype(F32)
        lat[pl.ds(image * tokens, tokens)] = jnp.concatenate(
            [out, jnp.zeros((tokens, LANES - HEAD), F32)], axis=1
        )

    attend(core)
    swap_back.wait()
    attend(1 - core)

    ext_ref[...] = jnp.zeros(ext_ref.shape, F32)
    line = 2 * SLOT

    def pack(pieces):
        packed = pieces[0]
        for i in range(1, HALO):
            packed = packed + pltpu.roll(pieces[i], i * HEAD, 1)
        return packed.astype(BF16)

    def rows_of(first):
        return pack([
            jnp.concatenate(
                [lat[i * tokens + (first + r) * tile : i * tokens + (first + r + 1) * tile] for i in range(2)],
                axis=0,
            )
            for r in range(HALO)
        ])

    def cols_of(first):
        return pack([lat[pl.ds(first + c, 2 * tile, stride=tile)] for c in range(HALO)])

    strips[0] = rows_of(0)
    strips[1] = rows_of(tile - HALO)
    strips[2] = cols_of(0)
    strips[3] = cols_of(tile - HALO)

    def exchange(d):
        dr, dc = AROUND[d]
        source = (0 if dr < 0 else 1) if dr else (2 if dc < 0 else 3)
        there = (
            (row + dr >= 0) & (row + dr < rows) & (col + dc >= 0) & (col + dc < cols)
        )
        return there, pltpu.make_async_remote_copy(
            src_ref=strips.at[source], dst_ref=halo.at[7 - d], send_sem=halo_send.at[d],
            recv_sem=halo_recv.at[7 - d], device_id=(row + dr, col + dc), device_id_type=MESH,
        )

    def exchange_from(d):
        dr, dc = AROUND[d]
        there = (
            (row + dr >= 0) & (row + dr < rows) & (col + dc >= 0) & (col + dc < cols)
        )
        return there, pltpu.make_async_remote_copy(
            src_ref=strips.at[0], dst_ref=halo.at[d], send_sem=halo_send.at[d],
            recv_sem=halo_recv.at[d], device_id=(row + dr, col + dc), device_id_type=MESH,
        )

    for d in range(8):
        there, copy = exchange(d)
        pl.when(there)(copy.start)

    for i in range(2):
        for y in range(tile):
            ext_ref[pl.ds((y + HALO) * line + i * SLOT + HALO, tile)] = lat[
                i * tokens + y * tile : i * tokens + (y + 1) * tile
            ]

    lane = lax.broadcasted_iota(jnp.int32, (2 * tile, LANES), 1)

    def take(d):
        dr, dc = AROUND[d]
        packed = halo[d].astype(F32)
        for n in range(HALO):
            piece = packed if n == 0 else pltpu.roll(packed, LANES - n * HEAD, 1)
            piece = jnp.where(lane < HEAD, piece, 0.0)
            for i in range(2):
                one = piece[i * tile : (i + 1) * tile]
                if dr:
                    y = n if dr < 0 else HALO + tile + n
                    at = y * line + i * SLOT
                    if dc < 0:
                        ext_ref[pl.ds(at, HALO)] = one[tile - HALO :]
                    elif dc == 0:
                        ext_ref[pl.ds(at + HALO, tile)] = one
                    else:
                        ext_ref[pl.ds(at + HALO + tile, HALO)] = one[:HALO]
                else:
                    x = n if dc < 0 else HALO + tile + n
                    ext_ref[pl.ds(HALO * line + i * SLOT + x, tile, stride=line)] = one

    for d in range(8):
        there, copy = exchange_from(d)

        @pl.when(there)
        def _(copy=copy, d=d):
            copy.wait_recv()
            take(d)

    each(lambda k: scatter(k).wait_send())
    each(lambda k: gather(k).wait_send())
    for d in range(8):
        there, copy = exchange(d)
        pl.when(there)(copy.wait_send)


def decoder_kernel(
    rows, cols, tile, ext_ref, entry_ref, gain_ref, res_ref, up_ref, out_ref,
    cat, hid, dec, ref_, shifted, sums, woven,
):
    row, col = lax.axis_index("row"), lax.axis_index("col")
    line = 2 * SLOT
    wide = tile + 2 * HALO
    chan = res_ref.shape[-1]

    def inside(reach, first, count):
        p = first + lax.broadcasted_iota(jnp.int32, (count, 1), 0)
        y, x = p // line - reach, lax.rem(lax.rem(p, line), SLOT) - reach
        gy, gx = row * tile + y, col * tile + x
        return (gy >= 0) & (gy < rows * tile) & (gx >= 0) & (gx < cols * tile)

    ext = ext_ref[...]
    n_ext = wide * line
    packed = ext
    for d in range(1, 3):
        packed = packed + pltpu.roll(pltpu.roll(ext, n_ext - d, 0), d * HEAD, 1)
    cat[...] = packed.astype(BF16)

    n_dec = (wide - 2) * line
    gain = gain_ref[...]
    half = n_dec // 2
    for part in range(2):
        lo = part * half
        acc = jnp.zeros((half, chan), F32)
        for dy in range(3):
            acc = acc + contract(
                cat[lo + dy * line : lo + dy * line + half, : 3 * HEAD], entry_ref[dy], 1, 0
            )
        value = acc.astype(BF16).astype(F32)
        dec[lo : lo + half] = value
        scaled = value * lax.rsqrt(jnp.mean(value * value, axis=1, keepdims=True) + NORM_EPS) * gain
        active = jnp.where(inside(2, lo, half), scaled * jax.nn.sigmoid(scaled), 0.0)
        hid[lo : lo + half, 0:chan] = active.astype(BF16)
    whole = hid[:, 0:chan].astype(F32)
    for d in range(1, 3):
        hid[:, d * chan : (d + 1) * chan] = pltpu.roll(whole, n_dec - d, 0).astype(BF16)

    n_ref = (wide - 4) * line
    tiles = 2
    step = n_ref // tiles
    rows_each = chan // tiles

    def residual(i, carry):
        lo = pl.multiple_of(i * step, 16)
        acc = jnp.zeros((step, chan), F32)
        for dy in range(3):
            acc = acc + contract(hid[pl.ds(pl.multiple_of(lo + dy * line, 16), step), :], res_ref[dy], 1, 0)
        center = pltpu.roll(dec[pl.ds(pl.multiple_of(lo + line, 8), step + 8), :], step + 7, 0)[:step]
        refined = (acc + center).astype(BF16).astype(F32)
        ref_[pl.ds(lo, step), :] = jnp.where(inside(1, lo, step), refined, 0.0)
        at = pl.ds(pl.multiple_of(i * rows_each, 16), rows_each)
        by_row = []
        for c in range(3):
            w = [up_ref[r, c, at, :].astype(F32) for r in range(3)]
            by_row.append((w[0], w[1] + w[2], w[0] + w[1], w[2]))
        for a in range(4):
            w = [by_row[c][a] for c in range(3)]
            for b, value in enumerate((w[0], w[1] + w[2], w[0] + w[1], w[2])):
                sums[a, b, at, :] = value.astype(BF16)
        return carry

    lax.fori_loop(0, tiles, residual, 0)

    for y in range(tile + 2):
        for i in range(2):
            part = ref_[y * line + i * SLOT : y * line + (i + 1) * SLOT]
            for d in range(3):
                moved = part if d == 0 else pltpu.roll(part, SLOT - d, 0)
                shifted[d, (y * 2 + i) * tile : (y * 2 + i + 1) * tile, :] = moved[:tile].astype(BF16)

    count = tile * 2 * tile
    for a in range(2):
        for b in range(2):
            acc = jnp.zeros((count, chan), F32)
            for di in range(2):
                for dj in range(2):
                    lo = (a + di) * 2 * tile
                    acc = acc + contract(
                        shifted[b + dj, lo : lo + count, :], sums[2 * a + di, 2 * b + dj], 1, 0
                    )
            for n in range(chan // LANES):
                woven[n, pl.ds(b, count, stride=2), :] = acc[:, n * LANES : (n + 1) * LANES]
        for n in range(chan // LANES):
            value = woven[n].astype(BF16).reshape(tile, 2, 2 * tile, LANES)
            for i in range(2):
                out_ref[i, :, a, :, n * LANES : (n + 1) * LANES] = value[:, i]


def local(rows, cols, q, k, v, proj, entry, gain, res, up):
    images, tile, _, width = q.shape
    chan = res.shape[-1]
    tokens = tile * tile
    chips = rows * cols // 2
    blocks = -(-width // LANES)
    per_chip = -(-(2 * blocks + -(-blocks // 16)) // chips)
    wide = tile + 2 * HALO
    line = 2 * SLOT
    vmem = pl.BlockSpec(memory_space=pltpu.VMEM)
    hbm = pl.BlockSpec(memory_space=pl.ANY)
    flat = (images, tokens, width)
    unit = (16, LANES)
    dma = pltpu.SemaphoreType.DMA
    ext = pl.pallas_call(
        functools.partial(attention_kernel, rows, cols, tile, width, per_chip),
        out_shape=jax.ShapeDtypeStruct((wide * line, LANES), F32),
        in_specs=[hbm] * 4,
        out_specs=vmem,
        scratch_shapes=[
            pltpu.VMEM(flat, BF16), pltpu.VMEM(flat, BF16), pltpu.VMEM(flat, BF16),
            pltpu.VMEM((proj.shape[1], width), BF16),
            pltpu.VMEM((images, chips * per_chip) + unit, F32),
            pltpu.VMEM((chips * per_chip,) + unit, F32),
            pltpu.VMEM((chips, per_chip) + unit, BF16),
            pltpu.VMEM((chips, per_chip) + unit, BF16),
            pltpu.VMEM((images, chips, per_chip) + unit, BF16),
            pltpu.VMEM((images * tokens, LANES), F32),
            pltpu.VMEM((4, 2 * tile, LANES), BF16),
            pltpu.VMEM((8, 2 * tile, LANES), BF16),
            dma((6,)), dma((4,)), dma((chips,)), dma((chips,)), dma((chips,)), dma((chips,)),
            dma((8,)), dma((8,)),
        ],
        compiler_params=pltpu.CompilerParams(
            collective_id=0, has_side_effects=True, vmem_limit_bytes=32 * 1024 * 1024
        ),
        name="attention",
    )(k.reshape(flat), v.reshape(flat), q.reshape(flat), proj.T)
    count = tile * 2 * tile
    out = pl.pallas_call(
        functools.partial(decoder_kernel, rows, cols, tile),
        out_shape=jax.ShapeDtypeStruct((images, tile, 2, 2 * tile, chan), BF16),
        in_specs=[vmem] * 5,
        out_specs=vmem,
        scratch_shapes=[
            pltpu.VMEM((wide * line, LANES), BF16),
            pltpu.VMEM(((wide - 2) * line, 3 * chan), BF16),
            pltpu.VMEM(((wide - 2) * line, chan), F32),
            pltpu.VMEM(((wide - 4) * line, chan), F32),
            pltpu.VMEM((3, (tile + 2) * 2 * tile, chan), BF16),
            pltpu.VMEM((4, 4, chan, chan), BF16),
            pltpu.VMEM((chan // LANES, 2 * count, LANES), F32),
        ],
        compiler_params=pltpu.CompilerParams(vmem_limit_bytes=44 * 1024 * 1024),
        name="decoder",
    )(ext, entry.reshape(3, -1, chan), gain.reshape(1, chan), res.reshape(3, -1, chan), up)
    return out.reshape(images, 2 * tile, 2 * tile, chan)


def solution(mesh):
    spread = P(None, "row", "col", None)
    rows, cols = mesh.shape["row"], mesh.shape["col"]
    return jax.shard_map(
        functools.partial(local, rows, cols),
        mesh=mesh,
        in_specs=(spread,) * 3 + (P(),) * 5,
        out_specs=spread,
        check_vma=False,
    )
```

profile of v0, /device:TPU:1, one launch (start us, length us, event | category | flops | bytes accessed | tf_op | source)
XLA Modules:
  0.0 53.0 jit_solution(10156169352908087910)
XLA Ops:
  0.0 0.0 copy-start.2
  0.0 1.7 %copy-done.2 = bf16[2,16,16,2240]{3,2,1,0:T(8,128)(2,1)S(1)} copy-done((bf16[2,16,16,2240]{3,2,1,0:T(8,128)(2,1)S(1)}, bf16[2,16,16,2240]{3,2,1,0:T(8,128)(2,1)}, u32[]{:S(2)}) %copy-start.2) | copy-done | bytes 2293784
  1.7 0.0 copy-start.3
  1.7 1.7 %copy-done.3 = bf16[2,16,16,2240]{3,2,1,0:T(8,128)(2,1)S(1)} copy-done((bf16[2,16,16,2240]{3,2,1,0:T(8,128)(2,1)S(1)}, bf16[2,16,16,2240]{3,2,1,0:T(8,128)(2,1)}, u32[]{:S(2)}) %copy-start.3) | copy-done | bytes 2293784
  3.3 0.0 copy-start.4
  3.3 1.7 %copy-done.4 = bf16[2,16,16,2240]{3,2,1,0:T(8,128)(2,1)S(1)} copy-done((bf16[2,16,16,2240]{3,2,1,0:T(8,128)(2,1)S(1)}, bf16[2,16,16,2240]{3,2,1,0:T(8,128)(2,1)}, u32[]{:S(2)}) %copy-start.4) | copy-done | bytes 2293784
  5.0 0.0 copy-start.6
  5.0 0.9 %copy-done.6 = bf16[2240,32]{0,1:T(8,128)(2,1)S(1)} copy-done((bf16[2240,32]{0,1:T(8,128)(2,1)S(1)}, bf16[2240,32]{0,1:T(8,128)(2,1)}, u32[]{:S(2)}) %copy-start.6) | copy-done | bytes 143384
  5.9 0.0 copy-start
  5.9 0.0 copy-start.5
  5.9 0.0 copy-start.7
  5.9 29.4 %attention.1.ext_ref = f32[1056,128]{1,0:T(8,128)S(1)} custom-call(bf16[2,256,2240]{2,1,0:T(8,128)(2,1)S(1)} %bitcast.9, bf16[2,256,2240]{2,1,0:T(8,128)(2,1)S(1)} %bitcast.10, bf16[2,256,2240]{2,1,0:T(8,128)(2,1)S(1)} %bitcast.11, bf16[32,2240]{1,0:T(8,128)(2,1)S(1)} %bitcast.13), custom_call_target="tpu_custom_call" | custom-call | tf_op jit(solution)/shard_map/attention/pallas_call | solution.py:398
  35.3 0.0 copy-done
  35.3 0.0 copy-done.5
  35.3 0.0 copy-done.7
  35.3 0.0 copy-start.1
  35.3 2.3 %copy-done.1 = bf16[3,3,512,512]{3,2,1,0:T(8,128)(2,1)S(1)} copy-done((bf16[3,3,512,512]{3,2,1,0:T(8,128)(2,1)S(1)}, bf16[3,3,512,512]{3,2,1,0:T(8,128)(2,1)}, u32[]{:S(2)}) %copy-start.1) | copy-done | bytes 4718616
  37.6 15.4 %decoder.1 = bf16[2,16,2,32,512]{4,3,2,1,0:T(8,128)(2,1)} custom-call(f32[1056,128]{1,0:T(8,128)S(1)} %attention.1.ext_ref, bf16[3,96,512]{2,1,0:T(8,128)(2,1)S(1)} %bitcast.12, f32[1,512]{1,0:T(1,128)S(1)} %bitcast.14, bf16[3,1536,512]{2,1,0:T(8,128)(2,1)S(1)} %bitcast.8, bf16[3,3,512,512]{3,2,1,0:T(8,128)(2,1)S(1)} %copy-done.1), custom_call_target="tpu_custom_call" | custom-call | tf_op jit(solution)/shard_map/decoder/pallas_call | solution.py:423
Async XLA Ops:
  0.0 1.7 %copy-start.2 = (bf16[2,16,16,2240]{3,2,1,0:T(8,128)(2,1)S(1)}, bf16[2,16,16,2240]{3,2,1,0:T(8,128)(2,1)}, u32[]{:S(2)}) copy-start(bf16[2,16,16,2240]{3,2,1,0:T(8,128)(2,1)} %param.9) | copy-start | bytes 6881284
  1.7 1.7 %copy-start.3 = (bf16[2,16,16,2240]{3,2,1,0:T(8,128)(2,1)S(1)}, bf16[2,16,16,2240]{3,2,1,0:T(8,128)(2,1)}, u32[]{:S(2)}) copy-start(bf16[2,16,16,2240]{3,2,1,0:T(8,128)(2,1)} %param.10) | copy-start | bytes 6881284
  3.3 1.7 %copy-start.4 = (bf16[2,16,16,2240]{3,2,1,0:T(8,128)(2,1)S(1)}, bf16[2,16,16,2240]{3,2,1,0:T(8,128)(2,1)}, u32[]{:S(2)}) copy-start(bf16[2,16,16,2240]{3,2,1,0:T(8,128)(2,1)} %param.8) | copy-start | bytes 6881284
  5.0 0.9 %copy-start.6 = (bf16[2240,32]{0,1:T(8,128)(2,1)S(1)}, bf16[2240,32]{0,1:T(8,128)(2,1)}, u32[]{:S(2)}) copy-start(bf16[2240,32]{0,1:T(8,128)(2,1)} %param.11) | copy-start | bytes 430084
  5.9 29.4 %copy-start = (bf16[3,3,512,512]{3,2,1,0:T(8,128)(2,1)S(1)}, bf16[3,3,512,512]{3,2,1,0:T(8,128)(2,1)}, u32[]{:S(2)}) copy-start(bf16[3,3,512,512]{3,2,1,0:T(8,128)(2,1)} %param.14) | copy-start | bytes 14155780
  5.9 29.4 %copy-start.5 = (bf16[3,3,32,512]{3,2,1,0:T(8,128)(2,1)S(1)}, bf16[3,3,32,512]{3,2,1,0:T(8,128)(2,1)}, u32[]{:S(2)}) copy-start(bf16[3,3,32,512]{3,2,1,0:T(8,128)(2,1)} %param.12) | copy-start | bytes 884740
  5.9 29.4 %copy-start.7 = (f32[512]{0:T(512)S(1)}, f32[512]{0:T(512)}, u32[]{:S(2)}) copy-start(f32[512]{0:T(512)} %param.13) | copy-start | bytes 6148
  35.3 2.3 %copy-start.1 = (bf16[3,3,512,512]{3,2,1,0:T(8,128)(2,1)S(1)}, bf16[3,3,512,512]{3,2,1,0:T(8,128)(2,1)}, u32[]{:S(2)}) copy-start(bf16[3,3,512,512]{3,2,1,0:T(8,128)(2,1)} %up_ref.1) | copy-start | bytes 14155780
where the time goes:
time: 53.6 us; the launch traced here: 53 us
  Pallas kernels  44.8 us (84%)
  local copies, waits for them, and re-layouts  8.25 us (15%)
    pallas_call x1, Pallas kernels, local(): pl.pallas_call(functools.partial(attention_kernel, rows, cols, tile, widt...  29.4 us
    pallas_call x1, Pallas kernels, local(): pl.pallas_call(functools.partial(decoder_kernel, rows, cols, tile), out_s...  15.4 us
    unnamed x16, local copies, waits for them, and re-layouts  8.25 us

commit v1 on v0

--- a/solution.py
+++ b/solution.py
@@ -32,7 +32,7 @@
     rows, cols, tile, width, per_chip,
     k_hbm, v_hbm, q_hbm, proj_hbm, ext_ref,
     k_buf, v_buf, q_buf, proj, part, other, chip_sum, arrived, total, lat, strips, halo,
-    in_sem, swap_sem, rs_send, rs_recv, ag_send, ag_recv, halo_send, halo_recv,
+    in_sem, swap_sem, rs_send, rs_recv, ag_send, ag_recv, halo_send, halo_recv, fw_send, fw_recv,
 ):
     row, col = lax.axis_index("row"), lax.axis_index("col")
     core = lax.rem(col, 2)
@@ -72,8 +72,11 @@
 
     lax.fori_loop(1, rows * cols, greet, 0)
 
-    units = chips * per_chip
-    part[:, 2 * blocks :] = jnp.zeros((2, units - 2 * blocks, 16, LANES), F32)
+    lead = -(-blocks // 16)
+    units = lead + 2 * blocks
+    owners = -(-units // per_chip)
+    part[:, :lead] = jnp.zeros((2, lead, 16, LANES), F32)
+    part[:, units:] = jnp.zeros((2, chips * per_chip - units, 16, LANES), F32)
     mask = same_head((LANES, LANES))
 
     def sums(image):
@@ -87,9 +90,11 @@
             for h in range(1, w // HEAD):
                 packed = packed + full[h * HEAD : (h + 1) * HEAD]
             mean = jnp.sum(keys.astype(F32), axis=0, keepdims=True)
-            part[image, 2 * b, :, 0:w] = packed[0:16]
-            part[image, 2 * b + 1, :, 0:w] = packed[16:32]
-            part[image, 2 * blocks + b // 16, b % 16 : b % 16 + 1, 0:w] = mean
+            if w < LANES:
+                packed = jnp.concatenate([packed, jnp.zeros((HEAD, LANES - w), F32)], axis=1)
+            part[image, lead + 2 * b] = packed[0:16]
+            part[image, lead + 2 * b + 1] = packed[16:32]
+            part[image, b // 16, b % 16 : b % 16 + 1, 0:w] = mean
 
     loads["k", 0].wait()
     loads["v", 0].wait()
@@ -127,13 +132,6 @@
             recv_sem=ag_recv.at[chip], device_id=place(t), device_id_type=MESH,
         )
 
-    def gather_from(k):
-        t = lax.rem(chip + k, chips)
-        return pltpu.make_async_remote_copy(
-            src_ref=total.at[core, t], dst_ref=total.at[core, t], send_sem=ag_send.at[k],
-            recv_sem=ag_recv.at[t], device_id=place(t), device_id_type=MESH,
-        )
-
     def each(body):
         def step(k, carry):
             body(k)
@@ -141,58 +139,82 @@
 
         lax.fori_loop(1, chips, step, 0)
 
-    each(lambda k: scatter(k).start())
+    def owner(k):
+        return lax.rem(chip + k, chips) < owners
+
+    each(lambda k: pl.when(owner(k))(scatter(k).start))
 
     def add(k, acc):
         t, copy = scatter_from(k)
         copy.wait_recv()
         return acc + arrived[t].astype(F32)
 
-    acc = lax.fori_loop(1, chips, add, chip_sum[chip].astype(F32))
-    total[core, chip] = (acc / token_count).astype(BF16)
-    each(lambda k: gather(k).start())
-    each(lambda k: gather_from(k).wait_recv())
-    swap_back = pltpu.make_async_remote_copy(
-        src_ref=total.at[core], dst_ref=total.at[core], send_sem=swap_sem.at[2],
-        recv_sem=swap_sem.at[3], device_id=partner, device_id_type=MESH,
-    )
-    swap_back.start()
+    def forward(t):
+        return pltpu.make_async_remote_copy(
+            src_ref=total.at[core, t], dst_ref=total.at[core, t], send_sem=fw_send.at[t],
+            recv_sem=fw_recv.at[t], device_id=partner, device_id_type=MESH,
+        )
+
+    def forwarded(t):
+        return pltpu.make_async_remote_copy(
+            src_ref=total.at[1 - core, t], dst_ref=total.at[1 - core, t], send_sem=fw_send.at[t],
+            recv_sem=fw_recv.at[t], device_id=partner, device_id_type=MESH,
+        )
+
+    @pl.when(chip < owners)
+    def _():
+        acc = lax.fori_loop(1, chips, add, chip_sum[chip].astype(F32))
+        total[core, chip] = (acc / token_count).astype(BF16)
+        each(lambda k: gather(k).start())
+
+    def receive(t):
+        @pl.when(chip != t)
+        def _():
+            pltpu.make_async_remote_copy(
+                src_ref=total.at[core, t], dst_ref=total.at[core, t], send_sem=ag_send.at[0],
+                recv_sem=ag_recv.at[t], device_id=place(t), device_id_type=MESH,
+            ).wait_recv()
+
+        forward(t).start()
+
+    def receive_forwarded(t):
+        forwarded(t).wait_recv()
+
     load_q.wait()
     load_proj.wait()
 
-    def unit(image, u, lo=0, hi=16):
-        return total[image, u // per_chip, u % per_chip]
-
-    def attend(image):
-        squares = jnp.zeros((tokens, 1), F32)
+    def attend(image, get):
+        squares = jnp.zeros((tokens, LANES), F32)
         out = jnp.zeros((tokens, HEAD), F32)
-        means = [
-            unit(image, 2 * blocks + i).astype(F32) for i in range(-(-blocks // 16))
-        ]
+        held = 0
+
+        def unit(u):
+            return total[image, u // per_chip, u % per_chip].astype(F32)
+
         for b in range(blocks):
+            while held * per_chip < lead + 2 * b + 2:
+                get(held)
+                held += 1
             lo = b * LANES
             w = min(LANES, width - lo)
-            packed = jnp.concatenate(
-                [unit(image, 2 * b).astype(F32), unit(image, 2 * b + 1).astype(F32)], axis=0
-            )
+            packed = jnp.concatenate([unit(lead + 2 * b), unit(lead + 2 * b + 1)], axis=0)
             spread = jnp.where(mask, jnp.concatenate([packed] * (LANES // HEAD), axis=0), 0.0)
-            mean = means[b // 16][b % 16 : b % 16 + 1]
+            mean = unit(b // 16)[b % 16 : b % 16 + 1]
             spread_mean = jnp.where(mask, jnp.broadcast_to(mean, (LANES, LANES)), 0.0)
             both = jnp.concatenate([spread, spread_mean], axis=0).astype(BF16)
             query = jnp.maximum(q_buf[image, :, lo : lo + w], 0)
             result = contract(query, both[:, :w], 1, 1)
-            attended = result[:, :w] / jnp.maximum(result[:, LANES : LANES + w], 1.0)
-            squares = squares + jnp.sum(attended * attended, axis=1, keepdims=True)
-            out = out + contract(attended.astype(BF16), proj[:, lo : lo + w], 1, 1)
-        out = out * lax.rsqrt(squares / width + NORM_EPS)
+            attended = result[:, :LANES] / jnp.maximum(result[:, LANES:], 1.0)
+            squares = squares + attended * attended
+            out = out + contract(attended[:, :w].astype(BF16), proj[:, lo : lo + w], 1, 1)
+        out = out * lax.rsqrt(jnp.sum(squares, axis=1, keepdims=True) / width + NORM_EPS)
         out = out.astype(BF16).astype(F32)
         lat[pl.ds(image * tokens, tokens)] = jnp.concatenate(
             [out, jnp.zeros((tokens, LANES - HEAD), F32)], axis=1
         )
 
-    attend(core)
-    swap_back.wait()
-    attend(1 - core)
+    attend(core, receive)
+    attend(1 - core, receive_forwarded)
 
     ext_ref[...] = jnp.zeros(ext_ref.shape, F32)
     line = 2 * SLOT
@@ -282,17 +304,21 @@
             copy.wait_recv()
             take(d)
 
-    each(lambda k: scatter(k).wait_send())
-    each(lambda k: gather(k).wait_send())
+    each(lambda k: pl.when(owner(k))(scatter(k).wait_send))
+    pl.when(chip < owners)(lambda: each(lambda k: gather(k).wait_send()))
+    for t in range(owners):
+        forward(t).wait_send()
     for d in range(8):
         there, copy = exchange(d)
         pl.when(there)(copy.wait_send)
 
 
 def decoder_kernel(
-    rows, cols, tile, ext_ref, entry_ref, gain_ref, res_ref, up_ref, out_ref,
-    cat, hid, dec, ref_, shifted, sums, woven,
+    rows, cols, tile, ext_ref, entry_ref, gain_ref, res_ref, up_hbm, out_ref,
+    up_ref, cat, hid, dec, ref_, shifted, sums, woven, up_sem,
 ):
+    load_up = pltpu.make_async_copy(up_hbm, up_ref, up_sem)
+    load_up.start()
     row, col = lax.axis_index("row"), lax.axis_index("col")
     line = 2 * SLOT
     wide = tile + 2 * HALO
@@ -354,6 +380,7 @@
                 sums[a, b, at, :] = value.astype(BF16)
         return carry
 
+    load_up.wait()
     lax.fori_loop(0, tiles, residual, 0)
 
     for y in range(tile + 2):
@@ -391,7 +418,7 @@
     wide = tile + 2 * HALO
     line = 2 * SLOT
     vmem = pl.BlockSpec(memory_space=pltpu.VMEM)
-    hbm = pl.BlockSpec(memory_space=pl.ANY)
+    hbm = pl.BlockSpec(memory_space=pltpu.HBM)
     flat = (images, tokens, width)
     unit = (16, LANES)
     dma = pltpu.SemaphoreType.DMA
@@ -411,21 +438,22 @@
             pltpu.VMEM((images * tokens, LANES), F32),
             pltpu.VMEM((4, 2 * tile, LANES), BF16),
             pltpu.VMEM((8, 2 * tile, LANES), BF16),
-            dma((6,)), dma((4,)), dma((chips,)), dma((chips,)), dma((chips,)), dma((chips,)),
-            dma((8,)), dma((8,)),
+            dma((6,)), dma((2,)), dma((chips,)), dma((chips,)), dma((chips,)), dma((chips,)),
+            dma((8,)), dma((8,)), dma((chips,)), dma((chips,)),
         ],
         compiler_params=pltpu.CompilerParams(
-            collective_id=0, has_side_effects=True, vmem_limit_bytes=32 * 1024 * 1024
+            collective_id=0, has_side_effects=True, vmem_limit_bytes=24 * 1024 * 1024
         ),
         name="attention",
-    )(k.reshape(flat), v.reshape(flat), q.reshape(flat), proj.T)
+    )(*(pltpu.with_memory_space_constraint(x, pltpu.HBM) for x in (k.reshape(flat), v.reshape(flat), q.reshape(flat), proj.T)))
     count = tile * 2 * tile
     out = pl.pallas_call(
         functools.partial(decoder_kernel, rows, cols, tile),
         out_shape=jax.ShapeDtypeStruct((images, tile, 2, 2 * tile, chan), BF16),
-        in_specs=[vmem] * 5,
+        in_specs=[vmem] * 4 + [hbm],
         out_specs=vmem,
         scratch_shapes=[
+            pltpu.VMEM(up.shape, BF16),
             pltpu.VMEM((wide * line, LANES), BF16),
             pltpu.VMEM(((wide - 2) * line, 3 * chan), BF16),
             pltpu.VMEM(((wide - 2) * line, chan), F32),
@@ -433,10 +461,11 @@
             pltpu.VMEM((3, (tile + 2) * 2 * tile, chan), BF16),
             pltpu.VMEM((4, 4, chan, chan), BF16),
             pltpu.VMEM((chan // LANES, 2 * count, LANES), F32),
+            dma,
         ],
-        compiler_params=pltpu.CompilerParams(vmem_limit_bytes=44 * 1024 * 1024),
+        compiler_params=pltpu.CompilerParams(vmem_limit_bytes=36 * 1024 * 1024),
         name="decoder",
-    )(ext, entry.reshape(3, -1, chan), gain.reshape(1, chan), res.reshape(3, -1, chan), up)
+    )(ext, entry.reshape(3, -1, chan), gain.reshape(1, chan), res.reshape(3, -1, chan), pltpu.with_memory_space_constraint(up, pltpu.HBM))
     return out.reshape(images, 2 * tile, 2 * tile, chan)
 
 

time: 53.6 us -> 47.2 us (0.88)
  local copies, waits for them, and re-layouts: 8.25 us -> 0.01 us
  Pallas kernels: 44.8 us -> 46.8 us
    unnamed x16 -> x6, local copies, waits for them, and re-layouts: 8.25 us -> 0.01 us
    pallas_call x1, Pallas kernels: 15.4 us -> 16.7 us  [local(): pl.pallas_call(functools.partial(decoder_kernel, rows, cols, tile), out_s...]
    pallas_call x1, Pallas kernels: 29.4 us -> 30.1 us  [local(): pl.pallas_call(functools.partial(attention_kernel, rows, cols, tile, widt...]
where the time goes in v1:
time: 47.2 us; the launch traced here: 47 us
  Pallas kernels  46.8 us (99%)
    pallas_call x1, Pallas kernels, local(): pl.pallas_call(functools.partial(attention_kernel, rows, cols, tile, widt...  30.1 us
    pallas_call x1, Pallas kernels, local(): pl.pallas_call(functools.partial(decoder_kernel, rows, cols, tile), out_s...  16.7 us

profile of v1, /device:TPU:1, one launch (start us, length us, event | category | flops | bytes accessed | tf_op | source)
XLA Modules:
  0.0 47.0 jit_solution(10636556629641123393)
XLA Ops:
  0.0 0.0 copy-start
  0.0 0.0 copy-start.1
  0.0 0.0 copy-start.2
  0.0 30.1 %attention.1.ext_ref = f32[1056,128]{1,0:T(8,128)S(1)} custom-call(bf16[2,256,2240]{2,1,0:T(8,128)(2,1)} %bitcast.11, bf16[2,256,2240]{2,1,0:T(8,128)(2,1)} %bitcast.12, bf16[2,256,2240]{2,1,0:T(8,128)(2,1)} %bitcast.13, bf16[32,2240]{1,0:T(8,128)(2,1)} %bitcast.14), custom_call_target="tpu_custom_call" | custom-call | tf_op jit(solution)/shard_map/attention/pallas_call | solution.py:425
  30.1 0.0 copy-done
  30.1 0.0 copy-done.1
  30.1 0.0 copy-done.2
  30.1 16.7 %decoder.1 = bf16[2,16,2,32,512]{4,3,2,1,0:T(8,128)(2,1)} custom-call(f32[1056,128]{1,0:T(8,128)S(1)} %attention.1.ext_ref, bf16[3,96,512]{2,1,0:T(8,128)(2,1)S(1)} %bitcast.9, f32[1,512]{1,0:T(1,128)S(1)} %bitcast.10, bf16[3,1536,512]{2,1,0:T(8,128)(2,1)S(1)} %bitcast.8, bf16[3,3,512,512]{3,2,1,0:T(8,128)(2,1)} %up_hbm.1), custom_call_target="tpu_custom_call" | custom-call | tf_op jit(solution)/shard_map/decoder/pallas_call | solution.py:450
Async XLA Ops:
  0.0 30.1 %copy-start = (bf16[3,3,512,512]{3,2,1,0:T(8,128)(2,1)S(1)}, bf16[3,3,512,512]{3,2,1,0:T(8,128)(2,1)}, u32[]{:S(2)}) copy-start(bf16[3,3,512,512]{3,2,1,0:T(8,128)(2,1)} %param.14) | copy-start | bytes 14155780
  0.0 30.1 %copy-start.1 = (bf16[3,3,32,512]{3,2,1,0:T(8,128)(2,1)S(1)}, bf16[3,3,32,512]{3,2,1,0:T(8,128)(2,1)}, u32[]{:S(2)}) copy-start(bf16[3,3,32,512]{3,2,1,0:T(8,128)(2,1)} %param.12) | copy-start | bytes 884740
  0.0 30.1 %copy-start.2 = (f32[512]{0:T(512)S(1)}, f32[512]{0:T(512)}, u32[]{:S(2)}) copy-start(f32[512]{0:T(512)} %param.13) | copy-start | bytes 6148

commit v2 on v1

--- a/solution.py
+++ b/solution.py
@@ -72,15 +72,19 @@
 
     lax.fori_loop(1, rows * cols, greet, 0)
 
-    lead = -(-blocks // 16)
-    units = lead + 2 * blocks
-    owners = -(-units // per_chip)
-    part[:, :lead] = jnp.zeros((2, lead, 16, LANES), F32)
-    part[:, units:] = jnp.zeros((2, chips * per_chip - units, 16, LANES), F32)
+    span = -(-blocks // 2)
+    groups = part.shape[2] // per_chip
+    used = 1 + 2 * span
+    part[:, :, 0:1] = jnp.zeros((2, 2, 1, 16, LANES), F32)
+    if part.shape[2] > used:
+        part[:, :, used:] = jnp.zeros((2, 2, part.shape[2] - used, 16, LANES), F32)
     mask = same_head((LANES, LANES))
 
-    def sums(image):
-        for b in range(blocks):
+    def of_half(half):
+        return range(half * span, min((half + 1) * span, blocks))
+
+    def sums(image, half):
+        for n, b in enumerate(of_half(half)):
             lo = b * LANES
             w = min(LANES, width - lo)
             keys = jnp.maximum(k_buf[image, :, lo : lo + w], 0)
@@ -92,129 +96,149 @@
             mean = jnp.sum(keys.astype(F32), axis=0, keepdims=True)
             if w < LANES:
                 packed = jnp.concatenate([packed, jnp.zeros((HEAD, LANES - w), F32)], axis=1)
-            part[image, lead + 2 * b] = packed[0:16]
-            part[image, lead + 2 * b + 1] = packed[16:32]
-            part[image, b // 16, b % 16 : b % 16 + 1, 0:w] = mean
-
-    loads["k", 0].wait()
-    loads["v", 0].wait()
-    sums(1 - core)
-    pl.semaphore_wait(barrier, rows * cols - 1)
-    swap = pltpu.make_async_remote_copy(
-        src_ref=part.at[1 - core], dst_ref=other, send_sem=swap_sem.at[0],
-        recv_sem=swap_sem.at[1], device_id=partner, device_id_type=MESH,
-    )
-    swap.start()
-    loads["k", 1].wait()
-    loads["v", 1].wait()
-    sums(core)
-    swap.wait()
-    chip_sum[...] = (part[core] + other[...]).reshape(chips, per_chip, 16, LANES).astype(BF16)
-
-    def scatter(k):
-        t = lax.rem(chip + k, chips)
+            part[image, half, 1 + 2 * n] = packed[0:16]
+            part[image, half, 2 + 2 * n] = packed[16:32]
+            part[image, half, 0, n : n + 1, 0:w] = mean
+
+    def swap(half):
         return pltpu.make_async_remote_copy(
-            src_ref=chip_sum.at[t], dst_ref=arrived.at[chip], send_sem=rs_send.at[k],
-            recv_sem=rs_recv.at[chip], device_id=place(t), device_id_type=MESH,
-        )
-
-    def scatter_from(k):
-        t = lax.rem(chip + k, chips)
-        return t, pltpu.make_async_remote_copy(
-            src_ref=chip_sum.at[t], dst_ref=arrived.at[t], send_sem=rs_send.at[k],
-            recv_sem=rs_recv.at[t], device_id=place(t), device_id_type=MESH,
-        )
-
-    def gather(k):
-        t = lax.rem(chip + k, chips)
-        return pltpu.make_async_remote_copy(
-            src_ref=total.at[core, chip], dst_ref=total.at[core, chip], send_sem=ag_send.at[k],
-            recv_sem=ag_recv.at[chip], device_id=place(t), device_id_type=MESH,
-        )
-
-    def each(body):
+            src_ref=part.at[1 - core, half], dst_ref=other.at[half], send_sem=swap_sem.at[half],
+            recv_sem=swap_sem.at[2 + half], device_id=partner, device_id_type=MESH,
+        )
+
+    def each(first, last, body):
         def step(k, carry):
             body(k)
             return carry
 
-        lax.fori_loop(1, chips, step, 0)
-
-    def owner(k):
-        return lax.rem(chip + k, chips) < owners
-
-    each(lambda k: pl.when(owner(k))(scatter(k).start))
-
-    def add(k, acc):
-        t, copy = scatter_from(k)
-        copy.wait_recv()
-        return acc + arrived[t].astype(F32)
-
-    def forward(t):
+        lax.fori_loop(first, last, step, 0)
+
+    def scatter(half, k):
+        g = lax.rem(chip // 2 + k, groups)
+        t = 2 * g + half
+        return t != chip, pltpu.make_async_remote_copy(
+            src_ref=chip_sum.at[half, g], dst_ref=arrived.at[chip], send_sem=rs_send.at[t],
+            recv_sem=rs_recv.at[chip], device_id=place(t), device_id_type=MESH,
+        )
+
+    def scatter_start(half, k):
+        away, copy = scatter(half, k)
+        pl.when(away)(copy.start)
+
+    def scatter_end(half, k):
+        away, copy = scatter(half, k)
+        pl.when(away)(copy.wait_send)
+
+    def owns(half):
+        return (lax.rem(chip, 2) == half) & (chip // 2 < groups)
+
+    def gather(half, k):
+        t = lax.rem(chip + k, chips)
+        mine = total.at[core, half, chip // 2]
         return pltpu.make_async_remote_copy(
-            src_ref=total.at[core, t], dst_ref=total.at[core, t], send_sem=fw_send.at[t],
-            recv_sem=fw_recv.at[t], device_id=partner, device_id_type=MESH,
-        )
-
-    def forwarded(t):
+            src_ref=mine, dst_ref=mine, send_sem=ag_send.at[k],
+            recv_sem=ag_recv.at[chip], device_id=place(t), device_id_type=MESH,
+        )
+
+    def reduce(half):
+        @pl.when(owns(half))
+        def _():
+            def add(k, acc):
+                t = lax.rem(chip + k, chips)
+                pltpu.make_async_remote_copy(
+                    src_ref=arrived.at[t], dst_ref=arrived.at[t], send_sem=rs_send.at[t],
+                    recv_sem=rs_recv.at[t], device_id=place(t), device_id_type=MESH,
+                ).wait_recv()
+                return acc + arrived[t].astype(F32)
+
+            acc = lax.fori_loop(1, chips, add, chip_sum[half, chip // 2].astype(F32))
+            total[core, half, chip // 2] = (acc / token_count).astype(BF16)
+            each(1, chips, lambda k: gather(half, k).start())
+
+    def collect(half):
+        def one(g):
+            t = 2 * g + half
+
+            @pl.when(t != chip)
+            def _():
+                chunk = total.at[core, half, g]
+                pltpu.make_async_remote_copy(
+                    src_ref=chunk, dst_ref=chunk, send_sem=ag_send.at[0],
+                    recv_sem=ag_recv.at[t], device_id=place(t), device_id_type=MESH,
+                ).wait_recv()
+
+        each(0, groups, one)
+        forward(half).start()
+
+    def forward(half):
         return pltpu.make_async_remote_copy(
-            src_ref=total.at[1 - core, t], dst_ref=total.at[1 - core, t], send_sem=fw_send.at[t],
-            recv_sem=fw_recv.at[t], device_id=partner, device_id_type=MESH,
-        )
-
-    @pl.when(chip < owners)
-    def _():
-        acc = lax.fori_loop(1, chips, add, chip_sum[chip].astype(F32))
-        total[core, chip] = (acc / token_count).astype(BF16)
-        each(lambda k: gather(k).start())
-
-    def receive(t):
-        @pl.when(chip != t)
-        def _():
-            pltpu.make_async_remote_copy(
-                src_ref=total.at[core, t], dst_ref=total.at[core, t], send_sem=ag_send.at[0],
-                recv_sem=ag_recv.at[t], device_id=place(t), device_id_type=MESH,
-            ).wait_recv()
-
-        forward(t).start()
-
-    def receive_forwarded(t):
-        forwarded(t).wait_recv()
-
+            src_ref=total.at[core, half], dst_ref=total.at[core, half], send_sem=fw_send.at[half],
+            recv_sem=fw_recv.at[half], device_id=partner, device_id_type=MESH,
+        )
+
+    def forwarded(half):
+        theirs = total.at[1 - core, half]
+        return pltpu.make_async_remote_copy(
+            src_ref=theirs, dst_ref=theirs, send_sem=fw_send.at[half],
+            recv_sem=fw_recv.at[half], device_id=partner, device_id_type=MESH,
+        )
+
+    loads["k", 0].wait()
+    loads["v", 0].wait()
+    sums(1 - core, 0)
+    pl.semaphore_wait(barrier, rows * cols - 1)
+    swap(0).start()
+    loads["k", 1].wait()
+    loads["v", 1].wait()
+    for half in range(2):
+        sums(core, half)
+        if half == 0:
+            sums(1 - core, 1)
+            swap(1).start()
+        swap(half).wait_recv()
+        chip_sum[half] = (
+            (part[core, half] + other[half]).reshape(chip_sum.shape[1:]).astype(BF16)
+        )
+        each(0, groups, functools.partial(scatter_start, half))
+    for half in range(2):
+        reduce(half)
     load_q.wait()
     load_proj.wait()
 
-    def attend(image, get):
-        squares = jnp.zeros((tokens, LANES), F32)
-        out = jnp.zeros((tokens, HEAD), F32)
-        held = 0
+    def attend(image, half, state):
+        squares, out = state
 
         def unit(u):
-            return total[image, u // per_chip, u % per_chip].astype(F32)
-
-        for b in range(blocks):
-            while held * per_chip < lead + 2 * b + 2:
-                get(held)
-                held += 1
+            return total[image, half, u // per_chip, u % per_chip].astype(F32)
+
+        means = unit(0)
+        for n, b in enumerate(of_half(half)):
             lo = b * LANES
             w = min(LANES, width - lo)
-            packed = jnp.concatenate([unit(lead + 2 * b), unit(lead + 2 * b + 1)], axis=0)
+            packed = jnp.concatenate([unit(1 + 2 * n), unit(2 + 2 * n)], axis=0)
             spread = jnp.where(mask, jnp.concatenate([packed] * (LANES // HEAD), axis=0), 0.0)
-            mean = unit(b // 16)[b % 16 : b % 16 + 1]
-            spread_mean = jnp.where(mask, jnp.broadcast_to(mean, (LANES, LANES)), 0.0)
+            spread_mean = jnp.where(mask, jnp.broadcast_to(means[n : n + 1], (LANES, LANES)), 0.0)
             both = jnp.concatenate([spread, spread_mean], axis=0).astype(BF16)
             query = jnp.maximum(q_buf[image, :, lo : lo + w], 0)
             result = contract(query, both[:, :w], 1, 1)
             attended = result[:, :LANES] / jnp.maximum(result[:, LANES:], 1.0)
             squares = squares + attended * attended
             out = out + contract(attended[:, :w].astype(BF16), proj[:, lo : lo + w], 1, 1)
+        return squares, out
+
+    start = (jnp.zeros((tokens, LANES), F32), jnp.zeros((tokens, HEAD), F32))
+    mine, theirs = start, start
+    for half in range(2):
+        collect(half)
+        mine = attend(core, half, mine)
+        forwarded(half).wait_recv()
+        theirs = attend(1 - core, half, theirs)
+    for image, (squares, out) in ((core, mine), (1 - core, theirs)):
         out = out * lax.rsqrt(jnp.sum(squares, axis=1, keepdims=True) / width + NORM_EPS)
         out = out.astype(BF16).astype(F32)
         lat[pl.ds(image * tokens, tokens)] = jnp.concatenate(
             [out, jnp.zeros((tokens, LANES - HEAD), F32)], axis=1
         )
-
-    attend(core, receive)
-    attend(1 - core, receive_forwarded)
 
     ext_ref[...] = jnp.zeros(ext_ref.shape, F32)
     line = 2 * SLOT
@@ -304,10 +328,13 @@
             copy.wait_recv()
             take(d)
 
-    each(lambda k: pl.when(owner(k))(scatter(k).wait_send))
-    pl.when(chip < owners)(lambda: each(lambda k: gather(k).wait_send()))
-    for t in range(owners):
-        forward(t).wait_send()
+    for half in range(2):
+        swap(half).wait_send()
+        forward(half).wait_send()
+        each(0, groups, functools.partial(scatter_end, half))
+        pl.when(owns(half))(
+            lambda half=half: each(1, chips, lambda k: gather(half, k).wait_send())
+        )
     for d in range(8):
         there, copy = exchange(d)
         pl.when(there)(copy.wait_send)
@@ -359,29 +386,27 @@
     n_ref = (wide - 4) * line
     tiles = 2
     step = n_ref // tiles
-    rows_each = chan // tiles
-
-    def residual(i, carry):
-        lo = pl.multiple_of(i * step, 16)
+
+    def residual(i):
+        lo = i * step
         acc = jnp.zeros((step, chan), F32)
         for dy in range(3):
-            acc = acc + contract(hid[pl.ds(pl.multiple_of(lo + dy * line, 16), step), :], res_ref[dy], 1, 0)
-        center = pltpu.roll(dec[pl.ds(pl.multiple_of(lo + line, 8), step + 8), :], step + 7, 0)[:step]
+            acc = acc + contract(hid[pl.ds(lo + dy * line, step), :], res_ref[dy], 1, 0)
+        center = pltpu.roll(dec[pl.ds(lo + line, step + 8), :], step + 7, 0)[:step]
         refined = (acc + center).astype(BF16).astype(F32)
         ref_[pl.ds(lo, step), :] = jnp.where(inside(1, lo, step), refined, 0.0)
-        at = pl.ds(pl.multiple_of(i * rows_each, 16), rows_each)
-        by_row = []
-        for c in range(3):
-            w = [up_ref[r, c, at, :].astype(F32) for r in range(3)]
-            by_row.append((w[0], w[1] + w[2], w[0] + w[1], w[2]))
-        for a in range(4):
-            w = [by_row[c][a] for c in range(3)]
-            for b, value in enumerate((w[0], w[1] + w[2], w[0] + w[1], w[2])):
-                sums[a, b, at, :] = value.astype(BF16)
-        return carry
-
+
+    residual(0)
     load_up.wait()
-    lax.fori_loop(0, tiles, residual, 0)
+    by_row = []
+    for c in range(3):
+        w = [up_ref[r, c].astype(F32) for r in range(3)]
+        by_row.append((w[0], w[1] + w[2], w[0] + w[1], w[2]))
+    for a in range(4):
+        w = [by_row[c][a] for c in range(3)]
+        for b, value in enumerate((w[0], w[1] + w[2], w[0] + w[1], w[2])):
+            sums[a, b] = value.astype(BF16)
+    residual(1)
 
     for y in range(tile + 2):
         for i in range(2):
@@ -414,7 +439,9 @@
     tokens = tile * tile
     chips = rows * cols // 2
     blocks = -(-width // LANES)
-    per_chip = -(-(2 * blocks + -(-blocks // 16)) // chips)
+    span = -(-blocks // 2)
+    per_chip = -(-(1 + 2 * span) // (chips // 2))
+    groups = -(-(1 + 2 * span) // per_chip)
     wide = tile + 2 * HALO
     line = 2 * SLOT
     vmem = pl.BlockSpec(memory_space=pltpu.VMEM)
@@ -430,16 +457,16 @@
         scratch_shapes=[
             pltpu.VMEM(flat, BF16), pltpu.VMEM(flat, BF16), pltpu.VMEM(flat, BF16),
             pltpu.VMEM((proj.shape[1], width), BF16),
-            pltpu.VMEM((images, chips * per_chip) + unit, F32),
-            pltpu.VMEM((chips * per_chip,) + unit, F32),
+            pltpu.VMEM((images, 2, groups * per_chip) + unit, F32),
+            pltpu.VMEM((2, groups * per_chip) + unit, F32),
+            pltpu.VMEM((2, groups, per_chip) + unit, BF16),
             pltpu.VMEM((chips, per_chip) + unit, BF16),
-            pltpu.VMEM((chips, per_chip) + unit, BF16),
-            pltpu.VMEM((images, chips, per_chip) + unit, BF16),
+            pltpu.VMEM((images, 2, groups, per_chip) + unit, BF16),
             pltpu.VMEM((images * tokens, LANES), F32),
             pltpu.VMEM((4, 2 * tile, LANES), BF16),
             pltpu.VMEM((8, 2 * tile, LANES), BF16),
-            dma((6,)), dma((2,)), dma((chips,)), dma((chips,)), dma((chips,)), dma((chips,)),
-            dma((8,)), dma((8,)), dma((chips,)), dma((chips,)),
+            dma((6,)), dma((4,)), dma((chips,)), dma((chips,)), dma((chips,)), dma((chips,)),
+            dma((8,)), dma((8,)), dma((2,)), dma((2,)),
         ],
         compiler_params=pltpu.CompilerParams(
             collective_id=0, has_side_effects=True, vmem_limit_bytes=24 * 1024 * 1024

time: 47.2 us -> 40 us (0.85)
  Pallas kernels: 46.8 us -> 39.7 us
    pallas_call x1, Pallas kernels: 16.7 us -> 12.8 us  [local(): pl.pallas_call(functools.partial(decoder_kernel, rows, cols, tile), out_s...]
    pallas_call x1, Pallas kernels: 30.1 us -> 26.8 us  [local(): pl.pallas_call(functools.partial(attention_kernel, rows, cols, tile, widt...]
where the time goes in v2:
time: 40 us; the launch traced here: 39.9 us
  Pallas kernels  39.7 us (99%)
    pallas_call x1, Pallas kernels, local(): pl.pallas_call(functools.partial(attention_kernel, rows, cols, tile, widt...  26.8 us
    pallas_call x1, Pallas kernels, local(): pl.pallas_call(functools.partial(decoder_kernel, rows, cols, tile), out_s...  12.8 us

profile of v2, /device:TPU:1, one launch (start us, length us, event | category | flops | bytes accessed | tf_op | source)
XLA Modules:
  0.0 39.9 jit_solution(10184631127057218041)
XLA Ops:
  0.0 0.0 copy-start
  0.0 0.0 copy-start.1
  0.0 0.0 copy-start.2
  0.0 26.8 %attention.1.ext_ref = f32[1056,128]{1,0:T(8,128)S(1)} custom-call(bf16[2,256,2240]{2,1,0:T(8,128)(2,1)} %bitcast.11, bf16[2,256,2240]{2,1,0:T(8,128)(2,1)} %bitcast.12, bf16[2,256,2240]{2,1,0:T(8,128)(2,1)} %bitcast.13, bf16[32,2240]{1,0:T(8,128)(2,1)} %bitcast.14), custom_call_target="tpu_custom_call" | custom-call | tf_op jit(solution)/shard_map/attention/pallas_call | solution.py:452
  26.9 0.0 copy-done
  26.9 0.0 copy-done.1
  26.9 0.0 copy-done.2
  26.9 12.8 %decoder.1 = bf16[2,16,2,32,512]{4,3,2,1,0:T(8,128)(2,1)} custom-call(f32[1056,128]{1,0:T(8,128)S(1)} %attention.1.ext_ref, bf16[3,96,512]{2,1,0:T(8,128)(2,1)S(1)} %bitcast.9, f32[1,512]{1,0:T(1,128)S(1)} %bitcast.10, bf16[3,1536,512]{2,1,0:T(8,128)(2,1)S(1)} %bitcast.8, bf16[3,3,512,512]{3,2,1,0:T(8,128)(2,1)} %up_hbm.1), custom_call_target="tpu_custom_call" | custom-call | tf_op jit(solution)/shard_map/decoder/pallas_call | solution.py:477
Async XLA Ops:
  0.0 26.9 %copy-start = (bf16[3,3,512,512]{3,2,1,0:T(8,128)(2,1)S(1)}, bf16[3,3,512,512]{3,2,1,0:T(8,128)(2,1)}, u32[]{:S(2)}) copy-start(bf16[3,3,512,512]{3,2,1,0:T(8,128)(2,1)} %param.14) | copy-start | bytes 14155780
  0.0 26.9 %copy-start.1 = (bf16[3,3,32,512]{3,2,1,0:T(8,128)(2,1)S(1)}, bf16[3,3,32,512]{3,2,1,0:T(8,128)(2,1)}, u32[]{:S(2)}) copy-start(bf16[3,3,32,512]{3,2,1,0:T(8,128)(2,1)} %param.12) | copy-start | bytes 884740
  0.0 26.9 %copy-start.2 = (f32[512]{0:T(512)S(1)}, f32[512]{0:T(512)}, u32[]{:S(2)}) copy-start(f32[512]{0:T(512)} %param.13) | copy-start | bytes 6148

commit v3 on v2

--- a/solution.py
+++ b/solution.py
@@ -191,10 +191,10 @@
     loads["k", 1].wait()
     loads["v", 1].wait()
     for half in range(2):
-        sums(core, half)
-        if half == 0:
+        if half == 1:
             sums(1 - core, 1)
             swap(1).start()
+        sums(core, half)
         swap(half).wait_recv()
         chip_sum[half] = (
             (part[core, half] + other[half]).reshape(chip_sum.shape[1:]).astype(BF16)
@@ -342,7 +342,7 @@
 
 def decoder_kernel(
     rows, cols, tile, ext_ref, entry_ref, gain_ref, res_ref, up_hbm, out_ref,
-    up_ref, cat, hid, dec, ref_, shifted, sums, woven, up_sem,
+    up_ref, cat, hid, dec, ref_, shifted, sums, woven, out_buf, up_sem, out_sem,
 ):
     load_up = pltpu.make_async_copy(up_hbm, up_ref, up_sem)
     load_up.start()
@@ -398,39 +398,50 @@
 
     residual(0)
     load_up.wait()
-    by_row = []
-    for c in range(3):
-        w = [up_ref[r, c].astype(F32) for r in range(3)]
-        by_row.append((w[0], w[1] + w[2], w[0] + w[1], w[2]))
-    for a in range(4):
-        w = [by_row[c][a] for c in range(3)]
-        for b, value in enumerate((w[0], w[1] + w[2], w[0] + w[1], w[2])):
-            sums[a, b] = value.astype(BF16)
+    taps = [[up_ref[r, c].astype(F32) for c in range(3)] for r in range(3)]
+    down = [taps[0][c] + taps[1][c] + taps[2][c] for c in range(3)]
+    sums[0] = (down[0] + down[1] + down[2]).astype(BF16)
+    for n in range(2):
+        sums[1 + n] = down[2 * n].astype(BF16)
+        sums[3 + n] = (taps[2 * n][0] + taps[2 * n][1] + taps[2 * n][2]).astype(BF16)
     residual(1)
 
     for y in range(tile + 2):
         for i in range(2):
             part = ref_[y * line + i * SLOT : y * line + (i + 1) * SLOT]
-            for d in range(3):
-                moved = part if d == 0 else pltpu.roll(part, SLOT - d, 0)
-                shifted[d, (y * 2 + i) * tile : (y * 2 + i + 1) * tile, :] = moved[:tile].astype(BF16)
+            center = pltpu.roll(part, SLOT - 1, 0)[:tile]
+            after = pltpu.roll(part, SLOT - 2, 0)[:tile]
+            at = slice((y * 2 + i) * tile, (y * 2 + i + 1) * tile)
+            shifted[0, at, :] = (part[:tile] - center).astype(BF16)
+            shifted[1, at, :] = center.astype(BF16)
+            shifted[2, at, :] = (after - center).astype(BF16)
 
     count = tile * 2 * tile
+    mid = slice(2 * tile, 2 * tile + count)
+
+    def row_step(field, a):
+        lo = 4 * a * tile
+        return (
+            shifted[field, lo : lo + count, :].astype(F32) - shifted[field, mid, :].astype(F32)
+        ).astype(BF16)
+
+    base = contract(shifted[1, mid, :], sums[0], 1, 0)
+    across = [base + contract(shifted[2 * b, mid, :], sums[1 + b], 1, 0) for b in range(2)]
+    stores = []
     for a in range(2):
+        along = contract(row_step(1, a), sums[3 + a], 1, 0)
         for b in range(2):
-            acc = jnp.zeros((count, chan), F32)
-            for di in range(2):
-                for dj in range(2):
-                    lo = (a + di) * 2 * tile
-                    acc = acc + contract(
-                        shifted[b + dj, lo : lo + count, :], sums[2 * a + di, 2 * b + dj], 1, 0
-                    )
+            acc = across[b] + along + contract(row_step(2 * b, a), up_ref[2 * a, 2 * b], 1, 0)
             for n in range(chan // LANES):
                 woven[n, pl.ds(b, count, stride=2), :] = acc[:, n * LANES : (n + 1) * LANES]
         for n in range(chan // LANES):
             value = woven[n].astype(BF16).reshape(tile, 2, 2 * tile, LANES)
             for i in range(2):
-                out_ref[i, :, a, :, n * LANES : (n + 1) * LANES] = value[:, i]
+                out_buf[a, i, :, :, n * LANES : (n + 1) * LANES] = value[:, i]
+        stores.append(pltpu.make_async_copy(out_buf.at[a], out_ref.at[:, :, a], out_sem.at[a]))
+        stores[-1].start()
+    for store in stores:
+        store.wait()
 
 
 def local(rows, cols, q, k, v, proj, entry, gain, res, up):
@@ -478,7 +489,7 @@
         functools.partial(decoder_kernel, rows, cols, tile),
         out_shape=jax.ShapeDtypeStruct((images, tile, 2, 2 * tile, chan), BF16),
         in_specs=[vmem] * 4 + [hbm],
-        out_specs=vmem,
+        out_specs=pl.BlockSpec(memory_space=pl.ANY),
         scratch_shapes=[
             pltpu.VMEM(up.shape, BF16),
             pltpu.VMEM((wide * line, LANES), BF16),
@@ -486,9 +497,11 @@
             pltpu.VMEM(((wide - 2) * line, chan), F32),
             pltpu.VMEM(((wide - 4) * line, chan), F32),
             pltpu.VMEM((3, (tile + 2) * 2 * tile, chan), BF16),
-            pltpu.VMEM((4, 4, chan, chan), BF16),
+            pltpu.VMEM((5, chan, chan), BF16),
             pltpu.VMEM((chan // LANES, 2 * count, LANES), F32),
+            pltpu.VMEM((2, images, tile, 2 * tile, chan), BF16),
             dma,
+            dma((2,)),
         ],
         compiler_params=pltpu.CompilerParams(vmem_limit_bytes=36 * 1024 * 1024),
         name="decoder",

time: 40 us -> 38.6 us (0.965)
  Pallas kernels: 39.7 us -> 38.2 us
    pallas_call x1, Pallas kernels: 12.8 us -> 11.4 us  [local(): pl.pallas_call(functools.partial(decoder_kernel, rows, cols, tile), out_s...]
where the time goes in v3:
time: 38.6 us; the launch traced here: 38.4 us
  Pallas kernels  38.2 us (99%)
    pallas_call x1, Pallas kernels, local(): pl.pallas_call(functools.partial(attention_kernel, rows, cols, tile, widt...  26.8 us
    pallas_call x1, Pallas kernels, local(): pl.pallas_call(functools.partial(decoder_kernel, rows, cols, tile), out_s...  11.4 us

profile of v3, /device:TPU:1, one launch (start us, length us, event | category | flops | bytes accessed | tf_op | source)
XLA Modules:
  0.0 38.4 jit_solution(5058050773015355838)
XLA Ops:
  0.0 0.0 copy-start
  0.0 0.0 copy-start.1
  0.0 0.0 copy-start.2
  0.0 26.8 %attention.1.ext_ref = f32[1056,128]{1,0:T(8,128)S(1)} custom-call(bf16[2,256,2240]{2,1,0:T(8,128)(2,1)} %bitcast.11, bf16[2,256,2240]{2,1,0:T(8,128)(2,1)} %bitcast.12, bf16[2,256,2240]{2,1,0:T(8,128)(2,1)} %bitcast.13, bf16[32,2240]{1,0:T(8,128)(2,1)} %bitcast.14), custom_call_target="tpu_custom_call" | custom-call | tf_op jit(solution)/shard_map/attention/pallas_call | solution.py:463
  26.9 0.0 copy-done
  26.9 0.0 copy-done.1
  26.9 0.0 copy-done.2
  26.9 11.4 %decoder.1 = bf16[2,16,2,32,512]{4,3,2,1,0:T(8,128)(2,1)} custom-call(f32[1056,128]{1,0:T(8,128)S(1)} %attention.1.ext_ref, bf16[3,96,512]{2,1,0:T(8,128)(2,1)S(1)} %bitcast.9, f32[1,512]{1,0:T(1,128)S(1)} %bitcast.10, bf16[3,1536,512]{2,1,0:T(8,128)(2,1)S(1)} %bitcast.8, bf16[3,3,512,512]{3,2,1,0:T(8,128)(2,1)} %up_hbm.1), custom_call_target="tpu_custom_call" | custom-call | tf_op jit(solution)/shard_map/decoder/pallas_call | solution.py:488
Async XLA Ops:
  0.0 26.9 %copy-start = (bf16[3,3,512,512]{3,2,1,0:T(8,128)(2,1)S(1)}, bf16[3,3,512,512]{3,2,1,0:T(8,128)(2,1)}, u32[]{:S(2)}) copy-start(bf16[3,3,512,512]{3,2,1,0:T(8,128)(2,1)} %param.14) | copy-start | bytes 14155780
  0.0 26.9 %copy-start.1 = (bf16[3,3,32,512]{3,2,1,0:T(8,128)(2,1)S(1)}, bf16[3,3,32,512]{3,2,1,0:T(8,128)(2,1)}, u32[]{:S(2)}) copy-start(bf16[3,3,32,512]{3,2,1,0:T(8,128)(2,1)} %param.12) | copy-start | bytes 884740
  0.0 26.9 %copy-start.2 = (f32[512]{0:T(512)S(1)}, f32[512]{0:T(512)}, u32[]{:S(2)}) copy-start(f32[512]{0:T(512)} %param.13) | copy-start | bytes 6148

commit v4 on v3

--- a/solution.py
+++ b/solution.py
@@ -58,8 +58,6 @@
     load_q = pltpu.make_async_copy(q_hbm, q_buf, in_sem.at[5])
     for copy in loads.values():
         copy.start()
-    load_proj.start()
-    load_q.start()
 
     barrier = pltpu.get_barrier_semaphore()
 
@@ -190,6 +188,8 @@
     swap(0).start()
     loads["k", 1].wait()
     loads["v", 1].wait()
+    load_proj.start()
+    load_q.start()
     for half in range(2):
         if half == 1:
             sums(1 - core, 1)

time: 38.6 us -> 38.6 us (level)
  no operation moved by 1% of the time
where the time goes in v4:
time: 38.6 us; the launch traced here: 38.4 us
  Pallas kernels  38.2 us (99%)
    pallas_call x1, Pallas kernels, local(): pl.pallas_call(functools.partial(attention_kernel, rows, cols, tile, widt...  26.8 us
    pallas_call x1, Pallas kernels, local(): pl.pallas_call(functools.partial(decoder_kernel, rows, cols, tile), out_s...  11.4 us

profile of v4, /device:TPU:1, one launch (start us, length us, event | category | flops | bytes accessed | tf_op | source)
XLA Modules:
  0.0 38.4 jit_solution(3049116618788746753)
XLA Ops:
  0.0 0.0 copy-start
  0.0 0.0 copy-start.1
  0.0 0.0 copy-start.2
  0.0 26.8 %attention.1.ext_ref = f32[1056,128]{1,0:T(8,128)S(1)} custom-call(bf16[2,256,2240]{2,1,0:T(8,128)(2,1)} %bitcast.11, bf16[2,256,2240]{2,1,0:T(8,128)(2,1)} %bitcast.12, bf16[2,256,2240]{2,1,0:T(8,128)(2,1)} %bitcast.13, bf16[32,2240]{1,0:T(8,128)(2,1)} %bitcast.14), custom_call_target="tpu_custom_call" | custom-call | tf_op jit(solution)/shard_map/attention/pallas_call | solution.py:463
  26.9 0.0 copy-done
  26.9 0.0 copy-done.1
  26.9 0.0 copy-done.2
  26.9 11.4 %decoder.1 = bf16[2,16,2,32,512]{4,3,2,1,0:T(8,128)(2,1)} custom-call(f32[1056,128]{1,0:T(8,128)S(1)} %attention.1.ext_ref, bf16[3,96,512]{2,1,0:T(8,128)(2,1)S(1)} %bitcast.9, f32[1,512]{1,0:T(1,128)S(1)} %bitcast.10, bf16[3,1536,512]{2,1,0:T(8,128)(2,1)S(1)} %bitcast.8, bf16[3,3,512,512]{3,2,1,0:T(8,128)(2,1)} %up_hbm.1), custom_call_target="tpu_custom_call" | custom-call | tf_op jit(solution)/shard_map/decoder/pallas_call | solution.py:488
Async XLA Ops:
  0.0 26.9 %copy-start = (bf16[3,3,512,512]{3,2,1,0:T(8,128)(2,1)S(1)}, bf16[3,3,512,512]{3,2,1,0:T(8,128)(2,1)}, u32[]{:S(2)}) copy-start(bf16[3,3,512,512]{3,2,1,0:T(8,128)(2,1)} %param.14) | copy-start | bytes 14155780
  0.0 26.9 %copy-start.1 = (bf16[3,3,32,512]{3,2,1,0:T(8,128)(2,1)S(1)}, bf16[3,3,32,512]{3,2,1,0:T(8,128)(2,1)}, u32[]{:S(2)}) copy-start(bf16[3,3,32,512]{3,2,1,0:T(8,128)(2,1)} %param.12) | copy-start | bytes 884740
  0.0 26.9 %copy-start.2 = (f32[512]{0:T(512)S(1)}, f32[512]{0:T(512)}, u32[]{:S(2)}) copy-start(f32[512]{0:T(512)} %param.13) | copy-start | bytes 6148
